TPU v7x, 32 devices: a whole 2x2x4 slice. The times are simulated.
32 devices in a mesh: seq: 16 (over z, y, core), head: 2 (over x).
Axes of the slice: x: 2, y: 2, z: 4, core: 2. Of those that a mesh axis runs over, the one named last changes fastest.
Arguments:
- queries: bfloat16 [11264, 8192], P('seq', 'head'), may hold values from -90 to 90
- encoded: bfloat16 [352, 32, 1024], P('seq', None, 'head'), may hold values from -6 to 6
- enc_gain: float32 [1024], P('head'), may hold values from 0.1 to 1.9
- w_kv: bfloat16 [1024, 2, 8192], P('seq', None, 'head'), may hold values from -0.1875 to 0.1875
- neighbour_block: int32 [352], replicated, may hold values from 0 to 175, as said below
- grad_context: bfloat16 [11264, 8192], P('seq', 'head'), may hold values from -6 to 6
Outputs:
- grad_queries: bfloat16 [11264, 8192], P('seq', 'head')
- grad_encoded: bfloat16 [352, 32, 1024], P('seq', None, 'head')
Inputs may be any that keep to these rules, and one draw needn't show every extreme that they name: `neighbour_block`: every query block has exactly 2 neighbours. The 22 neighbours of one shard of encoded go to 11 distinct owners of query blocks (block // 11), exactly 2 to each.
All inputs are finite; a program needn't handle non-finite values.
Results may differ from a plain program's by a relative error of at most 0.0065.
The roundings to bfloat16 on the way count: a program that leaves them out, or rounds other values in their place, can miss the bound.
Values may be sent and summed in bfloat16 or wider, within the bound.
A program may use at most 192 MiB of HBM per device.

v0:
```python
import jax
import jax.numpy as jnp
from jax import lax
from jax.sharding import PartitionSpec as P

HEAD_DIM = 128
SPAN = 64
NB = 2


def routing(neighbour_block, device, n_seq, per_dev, blocks_dev, slot_cap):
    count_all = neighbour_block.shape[0]
    index = jnp.arange(count_all, dtype=jnp.int32)
    source = index // per_dev
    holder = neighbour_block // blocks_dev
    earlier = index[None, :] < index[:, None]
    same_pair = jnp.logical_and(
        source[:, None] == source[None, :], holder[:, None] == holder[None, :]
    )
    slot_rank = jnp.sum(jnp.logical_and(same_pair, earlier), axis=1)
    block_rank = jnp.sum(
        jnp.logical_and(neighbour_block[:, None] == neighbour_block[None, :], earlier), axis=1
    )
    row_here = (neighbour_block - device * blocks_dev) * NB + block_rank
    mine_here = holder == device
    rows_local = jnp.arange(per_dev, dtype=jnp.int32)
    slots_all = jnp.arange(n_seq * slot_cap, dtype=jnp.int32)
    select_all = jnp.logical_and(
        rows_local[:, None] == row_here[None, :], mine_here[None, :]
    ).astype(jnp.bfloat16)
    slot_table = ((source * slot_cap + slot_rank)[:, None] == slots_all[None, :]).astype(
        jnp.bfloat16
    )
    recv_select = jnp.dot(select_all, slot_table, preferred_element_type=jnp.float32).astype(
        jnp.bfloat16
    )
    send_target = lax.dynamic_slice_in_dim(holder * slot_cap + slot_rank, device * per_dev, per_dev)
    send_select = (slots_all[:, None] == send_target[None, :]).astype(jnp.bfloat16)
    return (send_select, recv_select, select_all)


def shards(queries, encoded, enc_gain, w_kv, neighbour_block, grad_context):
    n_seq = lax.axis_size("seq")
    device = lax.axis_index("seq")
    per_dev, nlen, ew_part = encoded.shape
    ew_full = ew_part * lax.axis_size("head")
    tok_rows, d_part = queries.shape
    blocks_dev = tok_rows // SPAN
    heads_here = d_part // HEAD_DIM
    slot_cap = (per_dev + n_seq - 1) // n_seq
    scale = 1.0 / HEAD_DIM**0.5
    x_part = encoded.astype(jnp.float32)
    squares = lax.psum(jnp.sum(x_part * x_part, axis=-1), "head")
    inv_rms = lax.rsqrt(squares / ew_full + 1e-05)[..., None]
    normed = (x_part * inv_rms * enc_gain).astype(jnp.bfloat16)
    send_select, recv_select, select_all = routing(
        neighbour_block, device, n_seq, per_dev, blocks_dev, slot_cap
    )
    width_row = nlen * ew_part
    outgoing = jnp.dot(
        send_select, normed.reshape(per_dev, width_row), preferred_element_type=jnp.float32
    )
    outgoing = outgoing.astype(jnp.bfloat16).reshape(n_seq, slot_cap * width_row)
    incoming = lax.all_to_all(outgoing, "seq", split_axis=0, concat_axis=0, tiled=True)
    gathered = jnp.dot(
        recv_select,
        incoming.reshape(n_seq * slot_cap, width_row),
        preferred_element_type=jnp.float32,
    )
    owned = gathered.astype(jnp.bfloat16).reshape(per_dev, nlen, ew_part)
    full_rows = lax.all_gather(owned, "head", axis=2, tiled=True).reshape(per_dev * nlen, ew_full)
    weights = lax.all_gather(w_kv, "seq", axis=0, tiled=True)
    key_val = jnp.einsum(
        "re,ekd->rkd", full_rows, weights, preferred_element_type=jnp.float32
    ).astype(jnp.bfloat16)
    keys = key_val[:, 0, :].reshape(blocks_dev, NB * nlen, heads_here, HEAD_DIM)
    values = key_val[:, 1, :].reshape(blocks_dev, NB * nlen, heads_here, HEAD_DIM)
    q_heads = queries.reshape(blocks_dev, SPAN, heads_here, HEAD_DIM)
    scores = (
        jnp.einsum("cqhd,ckhd->chqk", q_heads, keys, preferred_element_type=jnp.float32) * scale
    )
    probs = jax.nn.softmax(scores, axis=-1)
    probs_low = probs.astype(jnp.bfloat16)
    g_heads = grad_context.reshape(blocks_dev, SPAN, heads_here, HEAD_DIM)
    dprobs = jnp.einsum("cqhd,ckhd->chqk", g_heads, values, preferred_element_type=jnp.float32)
    delta = jnp.sum(probs * dprobs, axis=-1, keepdims=True)
    dscores = (probs * (dprobs - delta)).astype(jnp.bfloat16)
    grad_queries = (
        jnp.einsum("chqk,ckhd->cqhd", dscores, keys, preferred_element_type=jnp.float32) * scale
    )
    grad_queries = grad_queries.astype(jnp.bfloat16).reshape(tok_rows, d_part)
    grad_keys = (
        jnp.einsum("chqk,cqhd->ckhd", dscores, q_heads, preferred_element_type=jnp.float32) * scale
    ).astype(jnp.bfloat16)
    grad_values = jnp.einsum(
        "chqk,cqhd->ckhd", probs_low, g_heads, preferred_element_type=jnp.float32
    ).astype(jnp.bfloat16)
    grad_kv = jnp.stack(
        [grad_keys.reshape(per_dev * nlen, d_part), grad_values.reshape(per_dev * nlen, d_part)],
        axis=1,
    )
    partial_rows = jnp.einsum("rkd,ekd->re", grad_kv, weights, preferred_element_type=jnp.float32)
    summed = lax.psum_scatter(
        partial_rows.reshape(per_dev, nlen, ew_full), "head", scatter_dimension=2, tiled=True
    )
    grad_owned = summed.astype(jnp.bfloat16).reshape(per_dev, width_row)
    returning = jnp.dot(recv_select.T, grad_owned, preferred_element_type=jnp.float32)
    returning = returning.astype(jnp.bfloat16).reshape(n_seq, slot_cap * width_row)
    arrived = lax.all_to_all(returning, "seq", split_axis=0, concat_axis=0, tiled=True)
    grad_normed = jnp.dot(
        send_select.T,
        arrived.reshape(n_seq * slot_cap, width_row),
        preferred_element_type=jnp.float32,
    )
    grad_normed = grad_normed.reshape(per_dev, nlen, ew_part)
    scaled = enc_gain * grad_normed
    inner = lax.psum(jnp.sum(x_part * scaled, axis=-1), "head")[..., None] / ew_full
    grad_encoded = (inv_rms * scaled - x_part * inv_rms * inv_rms * inv_rms * inner).astype(
        jnp.bfloat16
    )
    return (grad_queries, grad_encoded)


def solution(mesh):
    return jax.shard_map(
        shards,
        mesh=mesh,
        in_specs=(
            P("seq", "head"),
            P("seq", None, "head"),
            P("head"),
            P("seq", None, "head"),
            P(),
            P("seq", "head"),
        ),
        out_specs=(P("seq", "head"), P("seq", None, "head")),
        check_vma=False,
    )
```

profile of v0, /device:TPU:13, one launch (start us, length us, event | category | flops | bytes accessed | tf_op | source)
XLA Modules:
  0.0 522.2 jit_solution(16846907338019886596)
XLA Ops:
  7.2 0.7 broadcast_compare_fusion
  7.9 0.3 convert_reduce_fusion
  8.2 1.6 fusion.44
  9.7 6.1 %psum.14 = f32[22,32]{0,1:T(8,128)S(1)} all-reduce(f32[22,32]{0,1:T(8,128)S(1)} %fusion.44), channel_id=1, replica_groups=mesh['seq'=16,'head'=2] {'head'}, use_global_device_ids=true, to_apply=%region_3.4 | all-reduce | flops 704 | bytes 5632 | tf_op jit(solution)/shard_map/psum | solution.py:53
  15.9 1.6 fusion.39
  17.5 0.2 copy.72
  17.7 0.1 pad.2
  17.8 0.4 copy.91
  18.2 0.1 dynamic_slice.3
  18.3 0.5 convolution_convert_fusion.1
  18.9 1.6 all_to_all.16
  20.5 0.6 broadcast.100
  21.1 7.1 %reduce.2 = bf16[16,32768]{1,0:T(8,128)(2,1)S(1)} reduce(bf16[16,1,32768]{2,1,0:T(2,128)(2,1)S(1)} %all_to_all.16, bf16[]{:T(256)} %broadcast.100), dimensions={1}, to_apply=%all_to_all.16.reduce_sub_computation | reduce | bytes 2097154 | tf_op jit(solution)/shard_map/all_to_all | solution.py:64
  28.2 1.6 reshape.107
  29.8 8.6 %all-to-all-start = ((bf16[16,2,16384]{2,1,0:T(2,128)(2,1)}), bf16[16,2,16384]{2,1,0:T(2,128)(2,1)S(1)}, u32[]{:S(2)}, u32[]{:S(2)}) async-start(bf16[16,2,16384]{2,1,0:T(2,128)(2,1)} %reshape.107), calls=%async_computation | async-start | bytes 2097152 | tf_op jit(solution)/shard_map/all_to_all | solution.py:64
  38.4 0.3 all-gather.3.cloned.1.call-start
  38.7 0.2 convert_reduce_fusion.1
  38.9 0.2 convolution_convert_fusion.4
  39.1 24.1 %all-to-all-done = bf16[16,2,16384]{2,1,0:T(2,128)(2,1)S(1)} async-done(((bf16[16,2,16384]{2,1,0:T(2,128)(2,1)}), bf16[16,2,16384]{2,1,0:T(2,128)(2,1)S(1)}, u32[]{:S(2)}, u32[]{:S(2)}) %all-to-all-start) | async-done | bytes 1048608 | tf_op jit(solution)/shard_map/all_to_all | solution.py:64
  63.2 1.0 reshape.108
  64.3 6.4 %reduce = bf16[16,32768]{1,0:T(8,128)(2,1)S(1)} reduce(bf16[16,1,32768]{2,1,0:T(2,128)(2,1)S(1)} %reshape.108, bf16[]{:T(256)} %constant.44), dimensions={1}, to_apply=%all_to_all.13.reduce_sub_computation | reduce | bytes 2097154 | tf_op jit(solution)/shard_map/all_to_all | solution.py:64
  70.7 0.5 reshape.93
  71.1 0.4 convolution_convert_fusion.2
  71.5 0.2 copy.92
  71.8 0.9 slice.10
  72.8 1.6 copy.74
  74.4 7.1 %copy.94 = bf16[88,8,32,128]{3,2,1,0:T(8,128)(2,1)} copy(bf16[88,8,32,128]{3,1,2,0:T(8,128)(2,1)} %bitcast.97) | data formatting | bytes 11534336
  81.6 4.3 copy.96
  85.9 11.3 %all-gather.3.cloned.1.call-done = bf16[22,32,1024]{2,1,0:T(8,128)(2,1)} async-done(((bf16[22,32,512]{2,1,0:T(8,128)(2,1)}), bf16[22,32,1024]{2,1,0:T(8,128)(2,1)}) %all-gather.3.cloned.1.call-update) | async-done | bytes 1441808 | tf_op jit(solution)/shard_map/all_gather | solution.py:71
  97.2 127.3 %all-gather.5.cloned.1.call-done = bf16[1024,2,4096]{2,0,1:T(8,128)(2,1)} async-done(((bf16[64,2,4096]{2,0,1:T(8,128)(2,1)}), bf16[1024,2,4096]{2,0,1:T(8,128)(2,1)}) %all-gather.5.cloned.1.call-update) | async-done | bytes 16777232 | tf_op jit(solution)/shard_map/all_gather | solution.py:72
  224.5 29.4 %convolution_convert_fusion.3 = bf16[704,2,4096]{2,0,1:T(8,128)(2,1)} fusion(bf16[704,1024,1]{1,0,2:T(8,128)(2,1)} %bitcast.113, bf16[1024,2,4096]{2,0,1:T(8,128)(2,1)} %all-gather.5.cloned.1.call-done), kind=kOutput, calls=%fused_computation.20 | convolution fusion | flops 11816927232 | bytes 29753344 | tf_op jit(solution)/shard_map/re,ekd->rkd/dot_general | solution.py:73
  253.9 13.4 %slice_bitcast_fusion.1 = (bf16[88,8,32,128]{3,1,2,0:T(8,128)(2,1)}, bf16[88,8,32,128]{3,1,2,0:T(8,128)(2,1)}) fusion(bf16[704,2,4096]{2,0,1:T(8,128)(2,1)} %convolution_convert_fusion.3), kind=kLoop, calls=%fused_computation.25 | loop fusion | bytes 23068672
  267.3 4.5 copy.93
  271.8 2.4 copy-done
  274.3 10.5 %fusion.20 = f32[11,32,64,64]{3,2,1,0:T(8,128)} fusion(bf16[11,64,32,128]{3,2,1,0:T(8,128)(2,1)S(1)} %bitcast.90, bf16[11,64,32,128]{3,2,1,0:T(8,128)(2,1)} %bitcast.92), kind=kOutput, calls=%fused_computation.33 | convolution fusion | flops 369098752 | bytes 17301504 | tf_op jit(solution)/shard_map/cqhd,ckhd->chqk/dot_general | solution.py:80
  284.8 15.4 %fusion.65 = (f32[11,32,64]{2,1,0:T(8,128)S(1)}, f32[11,32,64,64]{2,3,1,0:T(8,128)}) fusion(f32[11,32,64,64]{3,2,1,0:T(8,128)} %fusion.20), kind=kOutput, calls=%fused_computation.92 | output fusion | flops 5767231 | bytes 11624448 | tf_op jit(solution)/shard_map/sub | solution.py:82
  300.2 4.6 copy.95
  304.8 11.7 %convert_bitcast_fusion = bf16[11,64,32,128]{3,1,2,0:T(8,128)(2,1)} fusion(bf16[11,64,32,128]{3,2,1,0:T(8,128)(2,1)} %bitcast.102, f32[11,32,64,64]{2,3,1,0:T(8,128)} %get-tuple-element.19, f32[11,32,64]{2,1,0:T(8,128)S(1)} %get-tuple-element.18), kind=kOutput, calls=%fused_computation.28 | convolution fusion | flops 374865920 | bytes 17391616 | tf_op jit(solution)/shard_map/chqk,cqhd->ckhd/dot_general | solution.py:95
  316.4 18.2 %fusion.5 = (f32[11,32,64]{2,1,0:T(8,128)S(1)}, f32[11,32,64,64]{3,2,1,0:T(8,128)}) fusion(f32[11,32,64,64]{2,3,1,0:T(8,128)} %get-tuple-element.19, f32[11,32,64]{2,1,0:T(8,128)S(1)} %get-tuple-element.18, bf16[11,64,32,128]{3,2,1,0:T(8,128)(2,1)} %bitcast.103, bf16[11,64,32,128]{3,2,1,0:T(8,128)(2,1)} %bitcast.104), kind=kOutput, calls=%fused_computation.10 | convolution fusion | flops 373401600 | bytes 23248896 | tf_op jit(solution)/shard_map/cqhd,ckhd->chqk/dot_general | solution.py:85
  334.6 9.8 %fusion.7 = bf16[11,32,64,64]{2,3,1,0:T(8,128)(2,1)S(1)} fusion(f32[11,32,64,64]{3,2,1,0:T(8,128)} %get-tuple-element.21, f32[11,32,64]{2,1,0:T(8,128)S(1)} %get-tuple-element.20, f32[11,32,64,64]{2,3,1,0:T(8,128)} %get-tuple-element.19, f32[11,32,64]{2,1,0:T(8,128)S(1)} %get-tuple-element.18), kind=kLoop, calls=%fused_computation.12 | loop fusion | flops 5767168 | bytes 14598144 | tf_op jit(solution)/shard_map/convert_element_type | solution.py:87
  344.4 7.3 %fusion.14 = bf16[11,64,32,128]{3,1,2,0:T(8,128)(2,1)S(1)} fusion(bf16[11,32,64,64]{2,3,1,0:T(8,128)(2,1)S(1)} %fusion.7, bf16[11,64,32,128]{3,2,1,0:T(8,128)(2,1)} %bitcast.93), kind=kOutput, calls=%fused_computation.22 | convolution fusion | flops 374865920 | bytes 14417920 | tf_op jit(solution)/shard_map/chqk,cqhd->ckhd/dot_general | solution.py:93
  351.8 6.9 %copy.83 = bf16[11,64,32,128]{3,2,1,0:T(8,128)(2,1)} copy(bf16[11,64,32,128]{3,1,2,0:T(8,128)(2,1)S(1)} %fusion.14) | data formatting | bytes 11534336 | tf_op jit(solution)/shard_map/convert_element_type | solution.py:94
  358.7 9.8 %stack_reshape.6 = bf16[704,1,4096]{2,0,1:T(8,128)(2,1)} reshape(bf16[11,64,32,128]{3,2,1,0:T(8,128)(2,1)} %copy.83) | data formatting | bytes 11534336 | tf_op jit(solution)/shard_map/stack;reshape | solution.py:98
  368.5 9.4 %copy.85 = bf16[11,64,32,128]{3,2,1,0:T(8,128)(2,1)} copy(bf16[11,64,32,128]{3,1,2,0:T(8,128)(2,1)} %convert_bitcast_fusion) | data formatting | bytes 11534336 | tf_op jit(solution)/shard_map/convert_element_type | solution.py:97
  377.9 9.7 %stack_reshape.7 = bf16[704,1,4096]{2,0,1:T(8,128)(2,1)} reshape(bf16[11,64,32,128]{3,2,1,0:T(8,128)(2,1)} %copy.85) | data formatting | bytes 11534336 | tf_op jit(solution)/shard_map/stack;reshape | solution.py:98
  387.6 20.1 %fusion.1 = f32[704,1024,1]{1,0,2:T(8,128)} fusion(bf16[1024,2,4096]{2,0,1:T(8,128)(2,1)} %all-gather.5.cloned.1.call-done, bf16[704,1,4096]{2,0,1:T(8,128)(2,1)} %stack_reshape.7, bf16[704,1,4096]{2,0,1:T(8,128)(2,1)} %stack_reshape.6), kind=kOutput, calls=%fused_computation.4 | convolution fusion | flops 11816927232 | bytes 31195136 | tf_op jit(solution)/shard_map/rkd,ekd->re/dot_general | solution.py:102
  407.7 41.2 %reduce-scatter.2.cloned.1.call-done = f32[22,32,512]{2,1,0:T(8,128)} async-done(((f32[22,32,1024]{2,1,0:T(8,128)}), f32[22,32,512]{2,1,0:T(8,128)}) %reduce-scatter.2.cloned.1.call-update) | async-done | bytes 1441808 | tf_op jit(solution)/shard_map/reduce_scatter | solution.py:103
  449.0 1.5 convert_element_type.76
  450.5 0.4 copy.98
  450.9 0.5 convolution_convert_fusion
  451.4 1.8 all_to_all.17
  453.3 7.1 %reduce.3 = bf16[16,32768]{1,0:T(8,128)(2,1)S(1)} reduce(bf16[16,1,32768]{2,1,0:T(2,128)(2,1)S(1)} %all_to_all.17, bf16[]{:T(256)} %broadcast.100), dimensions={1}, to_apply=%all_to_all.17.reduce_sub_computation | reduce | bytes 2097154 | tf_op jit(solution)/shard_map/all_to_all | solution.py:109
  460.3 1.6 reshape.109
  461.9 6.8 %all-to-all-start.1 = ((bf16[16,2,16384]{2,1,0:T(2,128)(2,1)}), bf16[16,2,16384]{2,1,0:T(2,128)(2,1)}, u32[]{:S(2)}, u32[]{:S(2)}) async-start(bf16[16,2,16384]{2,1,0:T(2,128)(2,1)} %reshape.109), calls=%async_computation.2 | async-start | bytes 2097152 | tf_op jit(solution)/shard_map/all_to_all | solution.py:109
  468.7 10.4 %fusion.13 = bf16[11,64,32,128]{3,1,2,0:T(8,128)(2,1)} fusion(bf16[11,32,64,64]{2,3,1,0:T(8,128)(2,1)} %copy-done.1, bf16[11,64,32,128]{3,2,1,0:T(8,128)(2,1)} %bitcast.91), kind=kOutput, calls=%fused_computation.21 | convolution fusion | flops 374865920 | bytes 14417920 | tf_op jit(solution)/shard_map/chqk,ckhd->cqhd/dot_general | solution.py:89
  479.1 7.0 %copy.81 = bf16[11,64,32,128]{3,2,1,0:T(8,128)(2,1)S(1)} copy(bf16[11,64,32,128]{3,1,2,0:T(8,128)(2,1)} %fusion.13) | data formatting | bytes 11534336 | tf_op jit(solution)/shard_map/convert_element_type | solution.py:91
  486.0 8.5 %copy.134 = bf16[88,8,32,128]{3,1,2,0:T(8,128)(2,1)} copy(bf16[88,8,32,128]{3,2,1,0:T(8,128)(2,1)S(1)} %bitcast.94) | data formatting | bytes 11534336
  494.5 4.4 reshape.110
  498.9 7.4 %reduce.1 = bf16[16,32768]{1,0:T(8,128)(2,1)} reduce(bf16[16,1,32768]{2,1,0:T(2,128)(2,1)S(1)} %reshape.110, bf16[]{:T(256)} %constant.44), dimensions={1}, to_apply=%all_to_all.15.reduce_sub_computation | reduce | bytes 2097154 | tf_op jit(solution)/shard_map/all_to_all | solution.py:109
  506.3 1.5 reshape.101
  507.8 0.8 fusion.45
  508.6 5.2 psum.15
  513.8 0.6 fusion.43
  514.4 1.1 copy.88
  (41 shorter events, 0.3 us)
Async XLA Ops:
  15.9 1.9 copy-start.4
  18.3 11.5 %copy-start.8 = (s32[22]{0:T(128)}, s32[22]{0:T(128)S(1)}, u32[]{:S(2)}) copy-start(s32[22]{0:T(128)S(1)} %dynamic_slice.3) | copy-start | bytes 268
  18.3 20.3 %copy-start.6 = (s32[352]{0:T(512)S(1)}, s32[352]{0:T(512)}, u32[]{:S(2)}) copy-start(s32[352]{0:T(512)} %param.10) | copy-start | bytes 4228
  29.8 33.5 %all-to-all-start = ((bf16[16,2,16384]{2,1,0:T(2,128)(2,1)}), bf16[16,2,16384]{2,1,0:T(2,128)(2,1)S(1)}, u32[]{:S(2)}, u32[]{:S(2)}) async-start(bf16[16,2,16384]{2,1,0:T(2,128)(2,1)} %reshape.107), calls=%async_computation | async-start | bytes 2097152 | tf_op jit(solution)/shard_map/all_to_all | solution.py:64
  38.4 58.8 %all-gather.3.cloned.1.call-start = ((), (), s32[]{:S(2)}) async-start(), calls=%async_computation.3 | async-start | bytes 2162688 | tf_op jit(solution)/shard_map/all_gather | solution.py:71
  70.7 2.1 copy-start.3
  72.7 151.7 %all-gather.5.cloned.1.call-start = ((), (), s32[]{:S(2)}) async-start(), calls=%async_computation.4 | async-start | bytes 17825792 | tf_op jit(solution)/shard_map/all_gather | solution.py:72
  74.4 7.2 %slice-start.2 = ((s8[5767168]{0:T(1024)(128)(4,1)}), s8[1572864]{0:T(1024)(128)(4,1)S(1)}, s32[]{:S(2)}) async-start(s8[5767168]{0:T(1024)(128)(4,1)} %bitcast.98), calls=%async_computation.8 | async-start | bytes 3145728
  74.4 374.6 %reduce-scatter.2.cloned.1.call-start = ((), (), s32[]{:S(2)}) async-start(), calls=%async_computation.5 | async-start | bytes 4325376 | tf_op jit(solution)/shard_map/reduce_scatter | solution.py:103
  74.4 7.1 %slice-start.3 = ((s8[5767168]{0:T(1024)(128)(4,1)}), s8[4194304]{0:T(1024)(128)(4,1)S(1)}, s32[]{:S(2)}) async-start(s8[5767168]{0:T(1024)(128)(4,1)} %bitcast.98), calls=%async_computation.9 | async-start | bytes 8388608
  271.8 2.4 copy-start
  274.3 25.9 %slice-start = ((s8[5767168]{0:T(1024)(128)(4,1)}), s8[1572864]{0:T(1024)(128)(4,1)S(1)}, s32[]{:S(2)}) async-start(s8[5767168]{0:T(1024)(128)(4,1)} %bitcast.95), calls=%async_computation.6 | async-start | bytes 3145728
  284.8 15.4 %slice-start.1 = ((s8[5767168]{0:T(1024)(128)(4,1)}), s8[4194304]{0:T(1024)(128)(4,1)S(1)}, s32[]{:S(2)}) async-start(s8[5767168]{0:T(1024)(128)(4,1)} %bitcast.95), calls=%async_computation.7 | async-start | bytes 8388608
  344.4 7.3 %copy-start.1 = (bf16[11,32,64,64]{2,3,1,0:T(8,128)(2,1)}, bf16[11,32,64,64]{2,3,1,0:T(8,128)(2,1)S(1)}, u32[]{:S(2)}) copy-start(bf16[11,32,64,64]{2,3,1,0:T(8,128)(2,1)S(1)} %fusion.7) | copy-start | bytes 8650756
  461.9 32.6 %all-to-all-start.1 = ((bf16[16,2,16384]{2,1,0:T(2,128)(2,1)}), bf16[16,2,16384]{2,1,0:T(2,128)(2,1)}, u32[]{:S(2)}, u32[]{:S(2)}) async-start(bf16[16,2,16384]{2,1,0:T(2,128)(2,1)} %reshape.109), calls=%async_computation.2 | async-start | bytes 2097152 | tf_op jit(solution)/shard_map/all_to_all | solution.py:109
  494.5 13.3 %copy-start.2 = (bf16[22,32,512]{2,1,0:T(8,128)(2,1)S(1)}, bf16[22,32,512]{2,1,0:T(8,128)(2,1)}, u32[]{:S(2)}) copy-start(bf16[22,32,512]{2,1,0:T(8,128)(2,1)} %param.7) | copy-start | bytes 2162692
  494.5 13.3 %copy-start.7 = (f32[512]{0:T(512)S(1)}, f32[512]{0:T(512)}, u32[]{:S(2)}) copy-start(f32[512]{0:T(512)} %param.8) | copy-start | bytes 6148
  494.5 13.3 %copy-start.9 = (s32[22]{0:T(128)S(1)}, s32[22]{0:T(128)}, u32[]{:S(2)}) copy-start(s32[22]{0:T(128)} %copy-done.8) | copy-start | bytes 268
  494.5 19.3 %copy-start.5 = (f32[22,32]{0,1:T(8,128)S(1)}, f32[22,32]{0,1:T(8,128)}, u32[]{:S(2)}) copy-start(f32[22,32]{0,1:T(8,128)} %copy-done.4) | copy-start | bytes 8452
Sparse Core Ops, SparseCore 0:
  72.9 24.2 all-gather.2
  100.0 124.4 all-gather.4
  407.8 41.0 reduce-scatter.1
where the time goes:
time: 530 us; the launch traced here: 522 us
  waiting for transfers between devices  204 us (38%)
  matrix products  110 us (21%)
  local copies, waits for them, and re-layouts  107 us (20%)
  other arithmetic  59.5 us (11%)
  starting transfers between devices  15.7 us (3%)
  between operations  14.3 us (3%)
  blocking collectives  11.3 us (2%)
    all_gather x1, waiting for transfers between devices, shards(): weights = lax.all_gather(w_kv, 'seq', axis=0, tiled=True)  127 us
    unnamed x45, local copies, waits for them, and re-layouts  57.4 us
    reduce_scatter x1, waiting for transfers between devices, shards(): lax.psum_scatter(partial_rows.reshape(per_dev, nlen, ew_full), 'head', sc...  41.2 us
    dot_general x1, matrix products, shards(): jnp.einsum('re,ekd->rkd', full_rows, weights, preferred_element_type=jnp....  29.4 us
    all_to_all x1, waiting for transfers between devices, shards(): lax.all_to_all(outgoing, 'seq', split_axis=0, concat_axis=0, tiled=True)  24.1 us
    dot_general x1, matrix products, shards(): jnp.einsum('rkd,ekd->re', grad_kv, weights, preferred_element_type=jnp.fl...  20.1 us
    another operation x2, local copies, waits for them, and re-layouts, shards(): jnp.stack([grad_keys.reshape(per_dev * nlen, d_part), grad_values.reshape...  19.5 us
    dot_general x1, matrix products, shards(): jnp.einsum('cqhd,ckhd->chqk', g_heads, values, preferred_element_type=jnp...  18.2 us
  transfers between devices with their start and end apart: 5, of which 4 were waited for; matrix products, arithmetic and copies ran while one was open for 8% of the time, Pallas kernels for 0%

commit v1 on v0

--- a/solution.py
+++ b/solution.py
@@ -1,6 +1,10 @@
+import functools
+
 import jax
 import jax.numpy as jnp
 from jax import lax
+from jax.experimental import pallas as pl
+from jax.experimental.pallas import tpu as pltpu
 from jax.sharding import PartitionSpec as P
 
 HEAD_DIM = 128
@@ -39,6 +43,182 @@
     return (send_select, recv_select, select_all)
 
 
+ACROSS = 4
+CORES = 2
+
+
+def gather_kernel(n, w_ref, out_ref, own_sem, send_sem, recv_sem):
+    me = lax.axis_index("seq")
+    wide = n // (ACROSS * CORES)
+    c = lax.rem(me, CORES)
+    b = lax.rem(me // CORES, wide)
+    a = me // (CORES * wide)
+
+    def at(aa, bb, cc):
+        return (aa * wide + bb) * CORES + cc
+
+    barrier = pltpu.get_barrier_semaphore()
+    partners = [at(lax.rem(a + 1, ACROSS), b, c), at(lax.rem(a + ACROSS - 1, ACROSS), b, c)]
+    partners.append(at(a, lax.rem(b + 1, wide), c))
+    if wide > 2:
+        partners.append(at(a, lax.rem(b + wide - 1, wide), c))
+    partners.append(at(a, b, 1 - c))
+    for partner in partners:
+        pl.semaphore_signal(
+            barrier, inc=1, device_id={"seq": partner}, device_id_type=pl.DeviceIdType.MESH
+        )
+    pl.semaphore_wait(barrier, len(partners))
+
+    def copy(slot, way, target, own):
+        return pltpu.make_async_remote_copy(
+            src_ref=w_ref if own else out_ref.at[slot],
+            dst_ref=out_ref.at[slot],
+            send_sem=send_sem.at[way, slot],
+            recv_sem=recv_sem.at[slot],
+            device_id={"seq": target},
+            device_id_type=pl.DeviceIdType.MESH,
+        )
+
+    def moves(aa, bb, from_a, from_b, own, act):
+        slot = at(aa, bb, c)
+        if from_b == 0:
+            if from_a >= 0:
+
+                @pl.when(a + 1 < ACROSS)
+                def _():
+                    act(copy(slot, 0, at(a + 1, b, c), own))
+
+            if from_a <= 0:
+
+                @pl.when(a > 0)
+                def _():
+                    act(copy(slot, 1, at(a - 1, b, c), own))
+
+        if from_b >= 0:
+
+            @pl.when(b + 1 < wide)
+            def _():
+                act(copy(slot, 2, at(a, b + 1, c), own))
+
+        if from_b <= 0:
+
+            @pl.when(b > 0)
+            def _():
+                act(copy(slot, 3, at(a, b - 1, c), own))
+
+        act(copy(slot, 4, at(a, b, 1 - c), own))
+
+    def start(item):
+        item.start()
+
+    def wait_recv(slot):
+        copy(slot, 4, at(a, b, 1 - c), False).wait_recv()
+
+    def visit(each):
+        for t in range(1, ACROSS + wide - 1):
+            for j in range(0, min(t, wide - 1) + 1):
+                k = t - j
+                if k > ACROSS - 1:
+                    continue
+                for sa in (1, -1) if k else (0,):
+                    for sb in (1, -1) if j else (0,):
+                        aa, bb = a - sa * k, b - sb * j
+                        here = None
+                        if sa:
+                            here = aa >= 0 if sa > 0 else aa < ACROSS
+                        if sb:
+                            more = bb >= 0 if sb > 0 else bb < wide
+                            here = more if here is None else jnp.logical_and(here, more)
+
+                        @pl.when(here)
+                        def _(aa=aa, bb=bb, sa=sa, sb=sb):
+                            each(aa, bb, sa, sb)
+
+    own_copy = pltpu.make_async_copy(w_ref, out_ref.at[me], own_sem)
+    moves(a, b, 0, 0, True, start)
+    own_copy.start()
+
+    def forward(aa, bb, sa, sb):
+        wait_recv(at(aa, bb, c))
+        moves(aa, bb, sa, sb, False, start)
+
+    visit(forward)
+    for aa in range(ACROSS):
+        for bb in range(wide):
+            wait_recv(at(aa, bb, 1 - c))
+    own_copy.wait()
+    moves(a, b, 0, 0, True, lambda item: item.wait_send())
+    visit(lambda aa, bb, sa, sb: moves(aa, bb, sa, sb, False, lambda item: item.wait_send()))
+
+
+def gather_weights(weights):
+    n = lax.axis_size("seq")
+    return pl.pallas_call(
+        functools.partial(gather_kernel, n),
+        out_shape=jax.ShapeDtypeStruct((n,) + weights.shape, weights.dtype),
+        in_specs=[pl.BlockSpec(memory_space=pl.ANY)],
+        out_specs=pl.BlockSpec(memory_space=pl.ANY),
+        scratch_shapes=[
+            pltpu.SemaphoreType.DMA,
+            pltpu.SemaphoreType.DMA((5, n)),
+            pltpu.SemaphoreType.DMA((n,)),
+        ],
+        compiler_params=pltpu.CompilerParams(collective_id=0, has_side_effects=True),
+    )(weights)
+
+
+GROUP = 4
+
+
+def attention_kernel(q_ref, g_ref, kv_ref, gq_ref, gkv_ref):
+    d_part = q_ref.shape[1]
+    scale = 1.0 / HEAD_DIM**0.5
+    nt = (((1,), (1,)), ((), ()))
+    tn = (((0,), (0,)), ((), ()))
+    dot = functools.partial(lax.dot_general, preferred_element_type=jnp.float32)
+
+    @pl.loop(0, d_part // (GROUP * HEAD_DIM))
+    def _(step):
+        for h in range(GROUP):
+            start = pl.multiple_of((step * GROUP + h) * HEAD_DIM, HEAD_DIM)
+            cols = pl.ds(start, HEAD_DIM)
+            cols_v = pl.ds(pl.multiple_of(start + d_part, HEAD_DIM), HEAD_DIM)
+            q, g = q_ref[:, cols], g_ref[:, cols]
+            k, v = kv_ref[:, cols], kv_ref[:, cols_v]
+            scores = dot(q, k, nt) * scale
+            weight = jnp.exp(scores - jnp.max(scores, axis=-1, keepdims=True))
+            probs = weight / jnp.sum(weight, axis=-1, keepdims=True)
+            dprobs = dot(g, v, nt)
+            delta = jnp.sum(probs * dprobs, axis=-1, keepdims=True)
+            dscores = (probs * (dprobs - delta)).astype(jnp.bfloat16)
+            low = probs.astype(jnp.bfloat16)
+            gq_ref[:, cols] = (jnp.dot(dscores, k, preferred_element_type=jnp.float32) * scale).astype(
+                jnp.bfloat16
+            )
+            gkv_ref[:, cols] = (dot(dscores, q, tn) * scale).astype(jnp.bfloat16)
+            gkv_ref[:, cols_v] = dot(low, g, tn).astype(jnp.bfloat16)
+
+
+def attention(queries, grads, kv):
+    rows, d_part = queries.shape
+    keys_rows = kv.shape[0] * SPAN // rows
+
+    def spec(height, width):
+        return pl.BlockSpec((height, width), lambda i: (i, 0))
+
+    return pl.pallas_call(
+        attention_kernel,
+        grid=(rows // SPAN,),
+        out_shape=(
+            jax.ShapeDtypeStruct(queries.shape, jnp.bfloat16),
+            jax.ShapeDtypeStruct(kv.shape, jnp.bfloat16),
+        ),
+        in_specs=[spec(SPAN, d_part), spec(SPAN, d_part), spec(keys_rows, 2 * d_part)],
+        out_specs=(spec(SPAN, d_part), spec(keys_rows, 2 * d_part)),
+        compiler_params=pltpu.CompilerParams(vmem_limit_bytes=40 * 1024 * 1024),
+    )(queries, grads, kv)
+
+
 def shards(queries, encoded, enc_gain, w_kv, neighbour_block, grad_context):
     n_seq = lax.axis_size("seq")
     device = lax.axis_index("seq")
@@ -46,9 +226,7 @@
     ew_full = ew_part * lax.axis_size("head")
     tok_rows, d_part = queries.shape
     blocks_dev = tok_rows // SPAN
-    heads_here = d_part // HEAD_DIM
     slot_cap = (per_dev + n_seq - 1) // n_seq
-    scale = 1.0 / HEAD_DIM**0.5
     x_part = encoded.astype(jnp.float32)
     squares = lax.psum(jnp.sum(x_part * x_part, axis=-1), "head")
     inv_rms = lax.rsqrt(squares / ew_full + 1e-05)[..., None]
@@ -69,37 +247,13 @@
     )
     owned = gathered.astype(jnp.bfloat16).reshape(per_dev, nlen, ew_part)
     full_rows = lax.all_gather(owned, "head", axis=2, tiled=True).reshape(per_dev * nlen, ew_full)
-    weights = lax.all_gather(w_kv, "seq", axis=0, tiled=True)
-    key_val = jnp.einsum(
-        "re,ekd->rkd", full_rows, weights, preferred_element_type=jnp.float32
-    ).astype(jnp.bfloat16)
-    keys = key_val[:, 0, :].reshape(blocks_dev, NB * nlen, heads_here, HEAD_DIM)
-    values = key_val[:, 1, :].reshape(blocks_dev, NB * nlen, heads_here, HEAD_DIM)
-    q_heads = queries.reshape(blocks_dev, SPAN, heads_here, HEAD_DIM)
-    scores = (
-        jnp.einsum("cqhd,ckhd->chqk", q_heads, keys, preferred_element_type=jnp.float32) * scale
-    )
-    probs = jax.nn.softmax(scores, axis=-1)
-    probs_low = probs.astype(jnp.bfloat16)
-    g_heads = grad_context.reshape(blocks_dev, SPAN, heads_here, HEAD_DIM)
-    dprobs = jnp.einsum("cqhd,ckhd->chqk", g_heads, values, preferred_element_type=jnp.float32)
-    delta = jnp.sum(probs * dprobs, axis=-1, keepdims=True)
-    dscores = (probs * (dprobs - delta)).astype(jnp.bfloat16)
-    grad_queries = (
-        jnp.einsum("chqk,ckhd->cqhd", dscores, keys, preferred_element_type=jnp.float32) * scale
-    )
-    grad_queries = grad_queries.astype(jnp.bfloat16).reshape(tok_rows, d_part)
-    grad_keys = (
-        jnp.einsum("chqk,cqhd->ckhd", dscores, q_heads, preferred_element_type=jnp.float32) * scale
-    ).astype(jnp.bfloat16)
-    grad_values = jnp.einsum(
-        "chqk,cqhd->ckhd", probs_low, g_heads, preferred_element_type=jnp.float32
-    ).astype(jnp.bfloat16)
-    grad_kv = jnp.stack(
-        [grad_keys.reshape(per_dev * nlen, d_part), grad_values.reshape(per_dev * nlen, d_part)],
-        axis=1,
-    )
-    partial_rows = jnp.einsum("rkd,ekd->re", grad_kv, weights, preferred_element_type=jnp.float32)
+    flat = w_kv.reshape(w_kv.shape[0], 2 * d_part)
+    weights = gather_weights(flat).reshape(ew_full, 2 * d_part)
+    kv = jnp.dot(full_rows, weights, preferred_element_type=jnp.float32).astype(jnp.bfloat16)
+    grad_queries, grad_kv = attention(queries, grad_context, kv)
+    partial_rows = lax.dot_general(
+        grad_kv, weights, (((1,), (1,)), ((), ())), preferred_element_type=jnp.float32
+    )
     summed = lax.psum_scatter(
         partial_rows.reshape(per_dev, nlen, ew_full), "head", scatter_dimension=2, tiled=True
     )

time: 530 us -> 503 us (0.949)
  the two profiles are of different devices: /device:TPU:13 before, /device:TPU:0 now
where the time goes in v1:
time: 503 us; the launch traced here: 495 us
  Pallas kernels  270 us (54%)
  waiting for transfers between devices  61.4 us (12%)
  blocking collectives  47.4 us (9%)
  matrix products  42.5 us (8%)
  other arithmetic  34.2 us (7%)
  local copies, waits for them, and re-layouts  18.3 us (4%)
  between operations  14.7 us (3%)
  starting transfers between devices  6.57 us (1%)
    pallas_call x1, Pallas kernels, attention(): pl.pallas_call(attention_kernel, grid=(rows // SPAN,), out_shape=(jax.Sha...  167 us
    pallas_call x1, Pallas kernels, gather_weights(): pl.pallas_call(functools.partial(gather_kernel, n), out_shape=jax.ShapeDt...  103 us
    reduce_scatter x1, waiting for transfers between devices, shards(): lax.psum_scatter(partial_rows.reshape(per_dev, nlen, ew_full), 'head', sc...  39.4 us
    all_to_all x1, blocking collectives, shards(): lax.all_to_all(returning, 'seq', split_axis=0, concat_axis=0, tiled=True)  30.5 us
    all_to_all x1, waiting for transfers between devices, shards(): lax.all_to_all(outgoing, 'seq', split_axis=0, concat_axis=0, tiled=True)  21.9 us
    dot_general x1, matrix products, shards(): jnp.dot(full_rows, weights, preferred_element_type=jnp.float32)  21 us
    dot_general x1, matrix products, shards(): lax.dot_general(grad_kv, weights, (((1,), (1,)), ((), ())), preferred_ele...  19 us
    all_to_all x2, other arithmetic, shards(): lax.all_to_all(returning, 'seq', split_axis=0, concat_axis=0, tiled=True)  14.4 us
  transfers between devices with their start and end apart: 3, of which 2 were waited for; matrix products, arithmetic and copies ran while one was open for 0% of the time, Pallas kernels for 21%

profile of v1, /device:TPU:0, one launch (start us, length us, event | category | flops | bytes accessed | tf_op | source)
XLA Modules:
  0.0 495.4 jit_solution(3566637911030325865)
XLA Ops:
  7.2 0.7 broadcast_compare_fusion
  7.9 0.3 convert_reduce_fusion
  8.2 1.6 fusion.7
  9.7 9.6 %psum.14 = f32[22,32]{0,1:T(8,128)S(1)} all-reduce(f32[22,32]{0,1:T(8,128)S(1)} %fusion.7), channel_id=1, replica_groups=mesh['seq'=16,'head'=2] {'head'}, use_global_device_ids=true, to_apply=%region_3.4 | all-reduce | flops 704 | bytes 5632 | tf_op jit(solution)/shard_map/psum | solution.py:231
  19.4 1.6 fusion.2
  21.0 0.2 copy.27
  21.2 0.1 pad
  21.3 0.4 copy.33
  21.7 0.1 dynamic_slice.3
  21.8 0.6 convolution_convert_fusion.1
  22.4 1.6 all_to_all.16
  24.0 0.5 broadcast.83
  24.5 7.0 %reduce.2 = bf16[16,32768]{1,0:T(8,128)(2,1)S(1)} reduce(bf16[16,1,32768]{2,1,0:T(2,128)(2,1)S(1)} %all_to_all.16, bf16[]{:T(256)} %broadcast.83), dimensions={1}, to_apply=%all_to_all.16.reduce_sub_computation | reduce | bytes 2097154 | tf_op jit(solution)/shard_map/all_to_all | solution.py:242
  31.5 1.6 reshape.97
  33.1 0.0 copy-start.3
  33.1 6.0 %all-to-all-start = ((bf16[16,2,16384]{2,1,0:T(2,128)(2,1)}), bf16[16,2,16384]{2,1,0:T(2,128)(2,1)S(1)}, u32[]{:S(2)}, u32[]{:S(2)}) async-start(bf16[16,2,16384]{2,1,0:T(2,128)(2,1)} %reshape.97), calls=%async_computation | async-start | bytes 2097152 | tf_op jit(solution)/shard_map/all_to_all | solution.py:242
  39.2 0.5 all-gather.2.cloned.1.call-start
  39.7 0.0 copy-done.3
  39.7 0.2 convert_reduce_fusion.1
  39.9 0.2 convolution_convert_fusion.4
  40.2 21.9 %all-to-all-done = bf16[16,2,16384]{2,1,0:T(2,128)(2,1)S(1)} async-done(((bf16[16,2,16384]{2,1,0:T(2,128)(2,1)}), bf16[16,2,16384]{2,1,0:T(2,128)(2,1)S(1)}, u32[]{:S(2)}, u32[]{:S(2)}) %all-to-all-start) | async-done | bytes 1048608 | tf_op jit(solution)/shard_map/all_to_all | solution.py:242
  62.1 1.0 reshape.98
  63.2 6.4 %reduce = bf16[16,32768]{1,0:T(8,128)(2,1)S(1)} reduce(bf16[16,1,32768]{2,1,0:T(2,128)(2,1)S(1)} %reshape.98, bf16[]{:T(256)} %constant.38), dimensions={1}, to_apply=%all_to_all.13.reduce_sub_computation | reduce | bytes 2097154 | tf_op jit(solution)/shard_map/all_to_all | solution.py:242
  69.5 0.5 reshape.86
  70.0 0.4 convolution_convert_fusion.2
  70.4 0.0 copy-start.2
  70.4 0.2 copy.34
  70.7 0.9 slice
  71.6 0.0 all-gather.2.cloned.1.call-update
  71.6 0.0 reduce-scatter.2.cloned.1.call-start
  71.7 0.0 copy-done.2
  71.7 1.6 copy.35
  73.2 0.0 slice-start
  73.2 103.3 %shard_map.77 = bf16[16,64,8192]{2,1,0:T(8,128)(2,1)} custom-call(bf16[64,8192]{1,0:T(8,128)(2,1)} %bitcast.42), custom_call_target="tpu_custom_call" | custom-call | tf_op jit(solution)/shard_map/pallas_call | solution.py:156
  176.6 0.0 all-gather.2.cloned.1.call-done
  176.6 0.0 slice-start.1
  176.6 21.0 %convolution_convert_fusion.3.kv_ref = bf16[704,8192]{1,0:T(8,128)(2,1)} fusion(bf16[704,1024]{1,0:T(8,128)(2,1)} %bitcast.51, bf16[1024,8192]{1,0:T(8,128)(2,1)} %bitcast.39), kind=kOutput, calls=%fused_computation.3 | convolution fusion | flops 11816927232 | bytes 29753344 | tf_op jit(solution)/shard_map/dot_general | solution.py:252
  197.6 0.0 slice-done
  197.6 0.0 slice-done.1
  197.6 0.0 copy-start
  197.6 2.6 copy-done
  200.3 167.0 %shard_map.78 = (bf16[704,4096]{1,0:T(8,128)(2,1)}, bf16[704,8192]{1,0:T(8,128)(2,1)}) custom-call(bf16[704,4096]{1,0:T(8,128)(2,1)S(1)} %bitcast.38, bf16[704,4096]{1,0:T(8,128)(2,1)S(1)} %copy-done, bf16[704,8192]{1,0:T(8,128)(2,1)} %convolution_convert_fusion.3.kv_ref), custom_call_target="tpu_custom_call" | custom-call | tf_op jit(solution)/shard_map/pallas_call | solution.py:209
  367.3 19.0 %fusion.26 = f32[22,32,1024]{2,1,0:T(8,128)} fusion(bf16[22,32,8192]{2,1,0:T(8,128)(2,1)} %bitcast.50, bf16[1024,8192,1]{1,0,2:T(8,128)(2,1)} %bitcast.40), kind=kOutput, calls=%fused_computation.52 | convolution fusion | flops 11811160064 | bytes 31195136 | tf_op jit(solution)/shard_map/dot_general | solution.py:254
  386.3 0.0 reduce-scatter.2.cloned.1.call-update
  386.3 39.4 %reduce-scatter.2.cloned.1.call-done = f32[22,32,512]{2,1,0:T(8,128)} async-done(((f32[22,32,1024]{2,1,0:T(8,128)}), f32[22,32,512]{2,1,0:T(8,128)}) %reduce-scatter.2.cloned.1.call-update) | async-done | bytes 1441808 | tf_op jit(solution)/shard_map/reduce_scatter | solution.py:257
  425.7 1.5 convert_element_type.44
  427.2 0.1 pad.1
  427.3 0.4 copy.36
  427.7 0.5 convolution_convert_fusion
  428.2 1.8 all_to_all.17
  430.0 7.0 %reduce.3 = bf16[16,32768]{1,0:T(8,128)(2,1)S(1)} reduce(bf16[16,1,32768]{2,1,0:T(2,128)(2,1)S(1)} %all_to_all.17, bf16[]{:T(256)} %broadcast.83), dimensions={1}, to_apply=%all_to_all.17.reduce_sub_computation | reduce | bytes 2097154 | tf_op jit(solution)/shard_map/all_to_all | solution.py:263
  437.0 0.8 reshape.99
  437.8 30.5 %all_to_all.20 = bf16[16,2,16384]{2,1,0:T(2,128)(2,1)S(1)} all-to-all(bf16[16,2,16384]{2,1,0:T(2,128)(2,1)S(1)} %reshape.99), channel_id=1, replica_groups=mesh['seq'=16,'head'=2] {'seq'}, dimensions={0} | all-to-all | bytes 2097152 | tf_op jit(solution)/shard_map/all_to_all | solution.py:263
  468.4 1.0 reshape.100
  469.4 7.4 %reduce.1 = bf16[16,32768]{1,0:T(8,128)(2,1)} reduce(bf16[16,1,32768]{2,1,0:T(2,128)(2,1)S(1)} %reshape.100, bf16[]{:T(256)} %constant.38), dimensions={1}, to_apply=%all_to_all.15.reduce_sub_computation | reduce | bytes 2097154 | tf_op jit(solution)/shard_map/all_to_all | solution.py:263
  476.8 0.0 copy-start.1
  476.8 0.0 copy-start.4
  476.8 1.6 reshape.92
  478.4 0.0 copy-done.1
  478.4 0.0 copy-done.4
  478.4 0.8 fusion.8
  479.2 7.2 %psum.15 = f32[22,32]{0,1:T(8,128)S(1)} all-reduce(f32[22,32]{0,1:T(8,128)S(1)} %get-tuple-element.20), channel_id=1, replica_groups=mesh['seq'=16,'head'=2] {'head'}, use_global_device_ids=true, to_apply=%region_6.7 | all-reduce | flops 704 | bytes 5632 | tf_op jit(solution)/shard_map/psum | solution.py:271
  486.4 0.6 fusion.6
  487.0 1.1 copy.31
  (6 shorter events, 0.1 us)
Async XLA Ops:
  33.1 6.5 %copy-start.3 = (s32[352]{0:T(512)S(1)}, s32[352]{0:T(512)}, u32[]{:S(2)}) copy-start(s32[352]{0:T(512)} %param.10) | copy-start | bytes 4228
  33.1 29.0 %all-to-all-start = ((bf16[16,2,16384]{2,1,0:T(2,128)(2,1)}), bf16[16,2,16384]{2,1,0:T(2,128)(2,1)S(1)}, u32[]{:S(2)}, u32[]{:S(2)}) async-start(bf16[16,2,16384]{2,1,0:T(2,128)(2,1)} %reshape.97), calls=%async_computation | async-start | bytes 2097152 | tf_op jit(solution)/shard_map/all_to_all | solution.py:242
  39.2 137.4 %all-gather.2.cloned.1.call-start = ((), (), s32[]{:S(2)}) async-start(), calls=%async_computation.3 | async-start | bytes 2162688 | tf_op jit(solution)/shard_map/all_gather | solution.py:249
  70.4 1.3 copy-start.2
  71.6 354.1 %reduce-scatter.2.cloned.1.call-start = ((), (), s32[]{:S(2)}) async-start(), calls=%async_computation.4 | async-start | bytes 4325376 | tf_op jit(solution)/shard_map/reduce_scatter | solution.py:257
  73.2 124.4 %slice-start = ((s8[5767168]{0:T(1024)(128)(4,1)}), s8[1572864]{0:T(1024)(128)(4,1)S(1)}, s32[]{:S(2)}) async-start(s8[5767168]{0:T(1024)(128)(4,1)} %bitcast.37), calls=%async_computation.5 | async-start | bytes 3145728
  176.6 21.0 %slice-start.1 = ((s8[5767168]{0:T(1024)(128)(4,1)}), s8[4194304]{0:T(1024)(128)(4,1)S(1)}, s32[]{:S(2)}) async-start(s8[5767168]{0:T(1024)(128)(4,1)} %bitcast.37), calls=%async_computation.6 | async-start | bytes 8388608
  197.6 2.6 copy-start
  476.8 1.6 copy-start.1
  476.8 1.6 copy-start.4
Sparse Core Ops, SparseCore 0:
  71.7 26.9 all-gather.1
  386.4 39.2 reduce-scatter.1
